TPU v7x, 32 devices: a whole 2x2x4 slice. The times are simulated.
32 devices in a mesh: wave: 8 (over z, x), lev: 4 (over y, core).
Axes of the slice: x: 2, y: 2, z: 4, core: 2. Of those that a mesh axis runs over, the one named last changes fastest.
Arguments:
- legendre_values: bfloat16 [1280, 64, 1280], P(('wave', 'lev')), may hold values from -0.15625 to 0.15625
- spectra: bfloat16 [1280, 1280, 128], P(('wave', 'lev')), may hold values from -0.16699219 to 0.16699219
- wave_table: int32 [1280], replicated, may hold values from 0 to 1279, each once
- row_longitudes: int32 [64], P(('wave', 'lev')), may hold values from 20 to 5136, as said below
Outputs:
- grid_fields: float32 [64, 64, 5376], P(('wave', 'lev'))
Inputs may be any that keep to these rules, and one draw needn't show every extreme that they name: `wave_table`: every wavenumber appears in exactly one slot. `row_longitudes`: each count is 20 plus a multiple of 4; some row of every draw has 5136.
All inputs are finite; a program needn't handle non-finite values.
Results may differ from a plain program's by a relative error of at most 0.0003.
Values sent between devices are 32-bit elements; how exact they have to be, the bound alone decides.
No kernel may reach another device: no remote copies, remote signals or barrier semaphores. Data moves between devices by JAX's collectives and lax.ppermute only.
A program may use at most 128 MiB of HBM per device.

v0:
```python
import jax
import jax.numpy as jnp
import numpy as np
from jax import lax
from jax.experimental import pallas as pl
from jax.experimental.pallas import tpu as pltpu
from jax.sharding import PartitionSpec as P

NLON = 5376
HALF = 256
SPAN = 2 * HALF
BLOCKS = -(-NLON // SPAN)
BLOCK_ROWS = 16
WHOLE = NLON // SPAN
SKIP = 16
PART = 8
GROUP = 5
TILE = 256
MB = 1 << 20


def fit_turns(function, odd):
    grid = np.cos(np.pi * (np.arange(4000) + 0.5) / 4000) * 0.13 + 0.1301
    roots = np.sqrt(grid)
    values = function(2 * np.pi * roots)
    if odd:
        values = values / roots
    fitted = np.polynomial.chebyshev.Chebyshev.fit(grid, values, 7)
    return [float(c) for c in fitted.convert(kind=np.polynomial.Polynomial).coef]


COS_TERMS = fit_turns(np.cos, False)
SIN_TERMS = fit_turns(np.sin, True)


def horner(terms, square):
    total = jnp.full_like(square, terms[-1])
    for term in terms[-2::-1]:
        total = total * square + term
    return total


def cos_sin(product, double_length, inverse):
    whole = jnp.floor(product * inverse + 0.5)
    turns = (product - whole * double_length) * inverse
    square = turns * turns
    return horner(COS_TERMS, square), horner(SIN_TERMS, square) * turns


def split(values):
    high = values.astype(jnp.bfloat16)
    low = (values - high.astype(jnp.float32)).astype(jnp.bfloat16)
    return high, low


def legendre_kernel(
    group, wave_in_ref, legendre_ref, spectra_ref, out_ref, wave_ref, values_ref, kept_ref, sums_ref,
    wave_sem, value_sems, in_sems, out_sems,
):
    slots, latitudes, degree_count = legendre_ref.shape
    block_number = lax.axis_index("wave") * lax.axis_size("lev") + lax.axis_index("lev")
    first_slot = block_number * slots
    wave_fetch = pltpu.make_async_copy(wave_in_ref, wave_ref, wave_sem)
    wave_fetch.start()

    def fetch(slot):
        first = pl.multiple_of(wave_ref[first_slot + slot] // SKIP * SKIP, SKIP)
        rows = pl.ds(first, degree_count - first)
        return (
            pltpu.make_async_copy(spectra_ref.at[slot, rows, :], kept_ref.at[slot, rows, :], in_sems.at[slot]),
        )

    def fetch_values(step):
        part = pl.ds(pl.multiple_of(step * group, group), group)
        return pltpu.make_async_copy(legendre_ref.at[part], values_ref.at[part], value_sems.at[step])

    def start_slot(slot, carry):
        for copy in fetch(slot):
            copy.start()
        return carry

    def send(step):
        first = pl.multiple_of(step * group, group)
        return pltpu.make_async_copy(sums_ref.at[step], out_ref.at[:, pl.ds(first, group), :], out_sems.at[step])

    degrees = lax.broadcasted_iota(jnp.int16, kept_ref.shape[1:], 0)

    def group_sums(step, carry):
        for first in range(0, group, PART):
            part = range(first, min(first + PART, group))
            if first == 0:
                fetch_values(step).wait()
            for index in part:
                for copy in fetch(step * group + index):
                    copy.wait()
            for index in part:
                slot = step * group + index
                wave = wave_ref[first_slot + slot]
                kept = jnp.where(degrees >= wave.astype(jnp.int16), kept_ref[slot], jnp.bfloat16(0))
                sums_ref[step, :, index, :] = jnp.dot(
                    values_ref[slot], kept, preferred_element_type=jnp.float32
                )
        send(step).start()
        return carry

    def finish_send(step, carry):
        send(step).wait()
        return carry

    fetch_values(0).start()
    wave_fetch.wait()
    for step in range(slots // group):
        if step:
            fetch_values(step).start()
        lax.fori_loop(step * group, step * group + group, start_slot, 0)
    lax.fori_loop(0, slots // group, group_sums, 0)
    lax.fori_loop(0, slots // group, finish_send, 0)


def legendre_stage(legendre_values, spectra, wave_table):
    slots, latitudes, degree_count = legendre_values.shape
    channels = spectra.shape[2]
    group = 8 if slots % 8 == 0 else slots
    return pl.pallas_call(
        lambda *refs: legendre_kernel(group, *refs),
        in_specs=[pl.BlockSpec(memory_space=pltpu.HBM)] * 3,
        out_specs=pl.BlockSpec(memory_space=pltpu.HBM),
        out_shape=jax.ShapeDtypeStruct((latitudes, slots, channels), jnp.float32),
        scratch_shapes=[
            pltpu.SMEM(wave_table.shape, wave_table.dtype),
            pltpu.VMEM((slots, latitudes, degree_count), jnp.bfloat16),
            pltpu.VMEM((slots, degree_count, channels), jnp.bfloat16),
            pltpu.VMEM((slots // group, latitudes, group, channels), jnp.float32),
            pltpu.SemaphoreType.DMA,
            pltpu.SemaphoreType.DMA((slots // group,)),
            pltpu.SemaphoreType.DMA((slots,)),
            pltpu.SemaphoreType.DMA((slots // group,)),
        ],
        compiler_params=pltpu.CompilerParams(vmem_limit_bytes=60 * MB),
        name="legendre",
    )(wave_table, legendre_values, spectra)


def table_kernel(length_ref, inverse_ref, lane_waves_ref, row_waves_ref, table_ref, turn_ref):
    row = pl.program_id(0)
    length = length_ref[row]
    inverse = inverse_ref[row]
    double_length = (2 * length).astype(jnp.float32)
    total_waves = row_waves_ref.shape[0]
    chunk = 64

    def fill(step, carry):
        first = pl.multiple_of(step * chunk, chunk)
        waves = row_waves_ref[pl.ds(first, chunk), :]
        for part in range(HALF // 128):
            lanes = lax.broadcasted_iota(jnp.int32, (chunk, 128), 1) + part * 128
            offsets = (2 * lanes + 1).astype(jnp.float32)
            values = cos_sin(waves * offsets, double_length, inverse)
            for kind in range(2):
                high, low = split(values[kind])
                table_ref[0, kind, 0, pl.ds(first, chunk), pl.ds(part * 128, 128)] = high
                table_ref[0, kind, 1, pl.ds(first, chunk), pl.ds(part * 128, 128)] = low
        return carry

    lax.fori_loop(0, total_waves // chunk, fill, 0)
    blocks = lax.broadcasted_iota(jnp.int32, (BLOCK_ROWS, total_waves), 0)
    centres = (2 * SPAN * blocks + (SPAN - 1)).astype(jnp.float32)
    waves = lane_waves_ref[0:1, :]
    turn_cos, turn_sin = cos_sin(waves * centres, double_length, inverse)
    limit = lax.shift_right_logical(length - 1, 1).astype(jnp.float32)
    weight = jnp.where(waves > limit, 0.0, jnp.where(waves == 0.0, 1.0, 2.0))
    turn_ref[0, 0] = turn_cos * weight
    turn_ref[0, 1] = turn_sin * weight


def table_stage(wave_table, row_longitudes):
    total_waves = wave_table.shape[0]
    local_rows = row_longitudes.shape[0]
    waves = wave_table.astype(jnp.float32)
    lane_waves = jnp.broadcast_to(waves[None, :], (8, total_waves))
    row_waves = jnp.broadcast_to(waves[:, None], (total_waves, 128))
    inverse = 0.5 / row_longitudes.astype(jnp.float32)
    entries = local_rows * total_waves * HALF
    return pl.pallas_call(
        table_kernel,
        grid=(local_rows,),
        in_specs=[
            pl.BlockSpec(memory_space=pltpu.SMEM),
            pl.BlockSpec(memory_space=pltpu.SMEM),
            pl.BlockSpec((8, total_waves), lambda i: (0, 0)),
            pl.BlockSpec((total_waves, 128), lambda i: (0, 0)),
        ],
        out_specs=[
            pl.BlockSpec((1, 2, 2, total_waves, HALF), lambda i: (i, 0, 0, 0, 0)),
            pl.BlockSpec((1, 2, BLOCK_ROWS, total_waves), lambda i: (i, 0, 0, 0)),
        ],
        out_shape=[
            pltpu.HBM((local_rows, 2, 2, total_waves, HALF), jnp.bfloat16),
            pltpu.HBM((local_rows, 2, BLOCK_ROWS, total_waves), jnp.float32),
        ],
        compiler_params=pltpu.CompilerParams(vmem_limit_bytes=32 * MB),
        cost_estimate=pl.CostEstimate(flops=entries * 40, bytes_accessed=entries * 8, transcendentals=0),
        name="trig_tables",
    )(row_longitudes, inverse, lane_waves, row_waves)


def fourier_kernel(
    length_in_ref, moved_in_ref, table_in_ref, turn_in_ref, out_ref,
    length_ref, moved_ref, table_ref, turn_ref, flipped_ref, real_ref, imag_ref, side_ref, result_ref,
    length_sem, in_sems, out_sems,
):
    senders, local_rows, slots, channels = moved_ref.shape
    total_waves = senders * slots
    fields = channels // 2
    length_fetch = pltpu.make_async_copy(length_in_ref, length_ref, length_sem)
    fetch_moved, fetch_turns, fetch_table = [], [], []
    for row in range(local_rows):
        fetch_moved.append(pltpu.make_async_copy(moved_in_ref.at[:, row], moved_ref.at[:, row], in_sems.at[row, 0]))
        fetch_turns.append(pltpu.make_async_copy(turn_in_ref.at[row], turn_ref.at[row], in_sems.at[row, 1]))
        fetch_table.append(pltpu.make_async_copy(table_in_ref.at[row], table_ref.at[row], in_sems.at[row, 2]))
    length_fetch.start()

    for row in range(local_rows):
        fetch_moved[row].start()

    def fetch_row(row):
        fetch_turns[row].start()
        fetch_table[row].start()

    fetch_row(0)

    def send(row, block):
        columns = pl.ds(pl.multiple_of(block * SPAN, SPAN), SPAN)
        return pltpu.make_async_copy(
            result_ref.at[row, :, columns], out_ref.at[row, :, columns], out_sems.at[row, block]
        )

    def send_last(row):
        columns = pl.ds(WHOLE * SPAN, NLON - WHOLE * SPAN)
        return pltpu.make_async_copy(
            result_ref.at[row, :, columns], out_ref.at[row, :, columns], out_sems.at[row, WHOLE]
        )

    def turn_row(row):
        moved = moved_ref[:, row].reshape(total_waves, channels)
        for step in range(total_waves // 128):
            lanes = slice(step * 128, (step + 1) * 128)
            flipped_ref[step] = moved[lanes].T
            real_ref[row, :, lanes] = flipped_ref[step, pl.ds(0, fields, stride=2), :]
            imag_ref[row, :, lanes] = flipped_ref[step, pl.ds(1, fields, stride=2), :]

    result_ref[...] = jnp.zeros_like(result_ref)
    reverse = 127 - lax.broadcasted_iota(jnp.int32, (fields, 128), 1)

    def rotate(row, first_block, count):
        for tile in range(total_waves // TILE):
            lanes = slice(tile * TILE, (tile + 1) * TILE)
            real = real_ref[row, :, lanes]
            imag = imag_ref[row, :, lanes]
            for index in range(count):
                turn_cos = turn_ref[row, 0, pl.ds(first_block + index, 1), lanes]
                turn_sin = turn_ref[row, 1, pl.ds(first_block + index, 1), lanes]
                sides = (real * turn_cos - imag * turn_sin, real * turn_sin + imag * turn_cos)
                for kind in range(2):
                    high, low = split(sides[kind])
                    side_ref[kind, index * fields : (index + 1) * fields, lanes] = high
                    side_ref[kind, (count + index) * fields : (count + index + 1) * fields, lanes] = low

    def transform(row, length, first_block, count):
        high_rows = count * fields
        sums = []
        for kind in range(2):
            piece = jnp.dot(
                side_ref[kind, : 2 * high_rows], table_ref[row, kind, 0], preferred_element_type=jnp.float32
            )
            rest = jnp.dot(side_ref[kind, :high_rows], table_ref[row, kind, 1], preferred_element_type=jnp.float32)
            sums.append(piece[:high_rows] + piece[high_rows:] + rest)
        for index in range(count):
            block = first_block + index
            even = sums[0][index * fields : (index + 1) * fields]
            odd = sums[1][index * fields : (index + 1) * fields]
            first = pl.multiple_of(block * SPAN, SPAN)
            below = even + odd
            parts = [below[:, p * 128 : (p + 1) * 128] for p in range(HALF // 128)]
            parts = [jnp.take_along_axis(part, reverse, axis=1) for part in parts[::-1]]
            below = jnp.concatenate(parts, axis=1)
            columns = lax.broadcasted_iota(jnp.int32, (fields, HALF), 1) + first
            result_ref[row, :, pl.ds(first, HALF)] = jnp.where(columns < length, below, 0.0)
            later = pl.multiple_of(first + HALF, HALF)
            result_ref[row, :, pl.ds(later, HALF)] = jnp.where(columns + HALF < length, even - odd, 0.0)

            @pl.when(block < WHOLE)
            def _():
                send(row, block).start()

    length_fetch.wait()
    for row in range(local_rows):
        length = length_ref[row]
        block_count = (length + SPAN - 1) // SPAN
        tail = lax.rem(block_count, GROUP) == 1
        group_count = jnp.where(tail, block_count // GROUP, (block_count + GROUP - 1) // GROUP)
        filled = jnp.minimum(group_count * GROUP + tail.astype(jnp.int32), WHOLE)

        def send_empty(block, carry):
            send(row, block).start()
            return carry

        lax.fori_loop(filled, WHOLE, send_empty, 0)
        if row == 0:
            for each in range(local_rows):
                fetch_moved[each].wait()
                turn_row(each)
        fetch_turns[row].wait()
        fetch_table[row].wait()
        if row + 1 < local_rows:
            fetch_row(row + 1)

        def one_group(group, carry):
            rotate(row, group * GROUP, GROUP)

            transform(row, length, group * GROUP, GROUP)
            return carry

        lax.fori_loop(0, group_count, one_group, 0)

        @pl.when(tail)
        def _():
            rotate(row, group_count * GROUP, 1)

            transform(row, length, group_count * GROUP, 1)

        send_last(row).start()

    for row in range(local_rows):
        for block in range(WHOLE):
            send(row, block).wait()
        send_last(row).wait()


def fourier_stage(moved, tables, turns, row_longitudes):
    senders, local_rows, slots, channels = moved.shape
    total_waves = senders * slots
    fields = channels // 2
    return pl.pallas_call(
        fourier_kernel,
        in_specs=[
            pl.BlockSpec(memory_space=pl.ANY),
            pl.BlockSpec(memory_space=pl.ANY),
            pl.BlockSpec(memory_space=pltpu.HBM),
            pl.BlockSpec(memory_space=pltpu.HBM),
        ],
        out_specs=pl.BlockSpec(memory_space=pltpu.HBM),
        out_shape=jax.ShapeDtypeStruct((local_rows, fields, NLON), jnp.float32),
        scratch_shapes=[
            pltpu.SMEM(row_longitudes.shape, row_longitudes.dtype),
            pltpu.VMEM(moved.shape, moved.dtype),
            pltpu.VMEM(tables.shape, tables.dtype),
            pltpu.VMEM(turns.shape, turns.dtype),
            pltpu.VMEM((total_waves // 128, channels, 128), jnp.float32),
            pltpu.VMEM((local_rows, fields, total_waves), jnp.float32),
            pltpu.VMEM((local_rows, fields, total_waves), jnp.float32),
            pltpu.VMEM((2, 2 * GROUP * fields, total_waves), jnp.bfloat16),
            pltpu.VMEM((local_rows, fields, (BLOCKS + GROUP) * SPAN), jnp.float32),
            pltpu.SemaphoreType.DMA,
            pltpu.SemaphoreType.DMA((local_rows, 3)),
            pltpu.SemaphoreType.DMA((local_rows, BLOCKS)),
        ],
        compiler_params=pltpu.CompilerParams(vmem_limit_bytes=50 * MB),
        name="fourier",
    )(row_longitudes, moved, tables, turns)


def per_device(legendre_values, spectra, wave_table, row_longitudes):
    slots = legendre_values.shape[0]
    devices = lax.axis_size("wave") * lax.axis_size("lev")
    local_rows = row_longitudes.shape[0]
    total_waves = wave_table.shape[0]
    sent = legendre_stage(legendre_values, spectra, wave_table)
    channels = sent.shape[2]
    moved = lax.all_to_all(
        sent.reshape(devices, local_rows * slots, channels), ("wave", "lev"), split_axis=0, concat_axis=0, tiled=True
    ).reshape(devices, local_rows, slots, channels)
    if slots % 8:
        moved = moved.swapaxes(0, 1).reshape(1, local_rows, devices * slots, channels)
    tables, turns = table_stage(wave_table, row_longitudes)
    return fourier_stage(moved, tables, turns, row_longitudes)


def solution(mesh):
    in_specs = (
        P(("wave", "lev"), None, None),
        P(("wave", "lev"), None, None),
        P(),
        P(("wave", "lev")),
    )
    out_specs = P(("wave", "lev"), None, None)
    return jax.shard_map(
        per_device, mesh=mesh, in_specs=in_specs, out_specs=out_specs, check_vma=False
    )
```

profile of v0, /device:TPU:2, one launch (start us, length us, event | category | flops | bytes accessed | tf_op | source)
XLA Modules:
  0.0 56.1 jit_solution(16817887712692067893)
XLA Ops:
  0.0 0.0 copy-start.2
  0.0 0.0 copy-start.1
  0.0 7.5 %legendre.1 = f32[64,40,128]{2,1,0:T(8,128)} custom-call(s32[1280]{0:T(1024)} %refs_0_.1, bf16[40,64,1280]{2,1,0:T(8,128)(2,1)} %refs_1_.1, bf16[40,1280,128]{2,1,0:T(8,128)(2,1)} %refs_2_.1), custom_call_target="tpu_custom_call" | custom-call | tf_op jit(solution)/shard_map/legendre/pallas_call | solution.py:124
  7.5 6.2 %all-to-all-start = ((f32[32,80,128]{2,1,0:T(8,128)}), f32[32,80,128]{2,1,0:T(8,128)S(1)}, u32[]{:S(2)}, u32[]{:S(2)}) async-start(f32[32,80,128]{2,1,0:T(8,128)} %bitcast.3), calls=%async_computation | async-start | bytes 2621440 | tf_op jit(solution)/shard_map/all_to_all | solution.py:380
  13.8 0.0 copy-done.2
  13.8 0.0 copy-done.1
  13.8 0.2 broadcast_in_dim.5.row_waves_ref
  14.1 6.7 %trig_tables.1 = (bf16[2,2,2,1280,256]{4,3,2,1,0:T(8,128)(2,1)}, f32[2,2,16,1280]{3,2,1,0:T(8,128)}) custom-call(s32[2]{0:T(128)S(1)} %copy-done.1, f32[2]{0:T(128)S(1)} %convert_divide_fusion.inverse_ref, f32[8,1280]{1,0:T(8,128)S(1)} %broadcast_in_dim.4.lane_waves_ref, f32[1280,128]{1,0:T(8,128)S(1)} %broadcast_in_dim.5.row_waves_ref), custom_call_target="tpu_custom_call" | custom-call | flops 26214400 | bytes 5242880 | tf_op jit(solution)/shard_map/trig_tables/pallas_call | solution.py:184
  20.8 24.5 %all-to-all-done = f32[32,80,128]{2,1,0:T(8,128)S(1)} async-done(((f32[32,80,128]{2,1,0:T(8,128)}), f32[32,80,128]{2,1,0:T(8,128)S(1)}, u32[]{:S(2)}, u32[]{:S(2)}) %all-to-all-start) | async-done | bytes 1310752 | tf_op jit(solution)/shard_map/all_to_all | solution.py:380
  45.3 0.0 copy-start
  45.3 1.0 %copy-done = f32[2,2,16,1280]{3,2,1,0:T(8,128)S(1)} copy-done((f32[2,2,16,1280]{3,2,1,0:T(8,128)S(1)}, f32[2,2,16,1280]{3,2,1,0:T(8,128)}, u32[]{:S(2)}) %copy-start) | copy-done | bytes 327704
  46.3 9.7 %fourier.1 = f32[2,64,5376]{2,1,0:T(8,128)} custom-call(s32[2]{0:T(128)S(1)} %copy-done.1, f32[32,2,40,128]{3,2,1,0:T(8,128)S(1)} %bitcast.2, bf16[2,2,2,1280,256]{4,3,2,1,0:T(8,128)(2,1)} %get-tuple-element.7.table_in_ref, f32[2,2,16,1280]{3,2,1,0:T(8,128)S(1)} %copy-done), custom_call_target="tpu_custom_call" | custom-call | tf_op jit(solution)/shard_map/fourier/pallas_call | solution.py:344
  (3 shorter events, 0.0 us)
Async XLA Ops:
  0.0 13.8 %copy-start.2 = (s32[1280]{0:T(1024)S(1)}, s32[1280]{0:T(1024)}, u32[]{:S(2)}) copy-start(s32[1280]{0:T(1024)} %refs_0_.1) | copy-start | bytes 15364
  0.0 13.8 %copy-start.1 = (s32[2]{0:T(128)S(1)}, s32[2]{0:T(128)}, u32[]{:S(2)}) copy-start(s32[2]{0:T(128)} %length_in_ref.1) | copy-start | bytes 28
  7.5 37.8 %all-to-all-start = ((f32[32,80,128]{2,1,0:T(8,128)}), f32[32,80,128]{2,1,0:T(8,128)S(1)}, u32[]{:S(2)}, u32[]{:S(2)}) async-start(f32[32,80,128]{2,1,0:T(8,128)} %bitcast.3), calls=%async_computation | async-start | bytes 2621440 | tf_op jit(solution)/shard_map/all_to_all | solution.py:380
  45.3 1.0 %copy-start = (f32[2,2,16,1280]{3,2,1,0:T(8,128)S(1)}, f32[2,2,16,1280]{3,2,1,0:T(8,128)}, u32[]{:S(2)}) copy-start(f32[2,2,16,1280]{3,2,1,0:T(8,128)} %get-tuple-element.8.turn_in_ref) | copy-start | bytes 983044
where the time goes:
time: 56.7 us; the launch traced here: 56.1 us
  waiting for transfers between devices  24.5 us (43%)
  Pallas kernels  24 us (42%)
  starting transfers between devices  6.24 us (11%)
  local copies, waits for them, and re-layouts  1.21 us (2%)
    all_to_all x1, waiting for transfers between devices, per_device(): lax.all_to_all(sent.reshape(devices, local_rows * slots, channels), ('wav...  24.5 us
    pallas_call x1, Pallas kernels, fourier_stage(): pl.pallas_call(fourier_kernel, in_specs=[pl.BlockSpec(memory_space=pl.ANY...  9.75 us
    pallas_call x1, Pallas kernels, legendre_stage(): pl.pallas_call(lambda *refs: legendre_kernel(group, *refs), in_specs=[pl....  7.53 us
    pallas_call x1, Pallas kernels, table_stage(): pl.pallas_call(table_kernel, grid=(local_rows,), in_specs=[pl.BlockSpec(m...  6.75 us
    all_to_all x1, starting transfers between devices, per_device(): lax.all_to_all(sent.reshape(devices, local_rows * slots, channels), ('wav...  6.24 us
  transfers between devices with their start and end apart: 1, of which 1 were waited for; matrix products, arithmetic and copies ran while one was open for 0% of the time, Pallas kernels for 12%

commit v1 on v0

--- a/solution.py
+++ b/solution.py
@@ -365,9 +365,14 @@
             pltpu.SemaphoreType.DMA((local_rows, 3)),
             pltpu.SemaphoreType.DMA((local_rows, BLOCKS)),
         ],
-        compiler_params=pltpu.CompilerParams(vmem_limit_bytes=50 * MB),
+        compiler_params=pltpu.CompilerParams(vmem_limit_bytes=36 * MB),
         name="fourier",
-    )(row_longitudes, moved, tables, turns)
+    )(
+        row_longitudes,
+        moved,
+        pltpu.with_memory_space_constraint(tables, pltpu.HBM),
+        pltpu.with_memory_space_constraint(turns, pltpu.HBM),
+    )
 
 
 def per_device(legendre_values, spectra, wave_table, row_longitudes):

time: 56.7 us -> 55.7 us (0.982)
  the two profiles are of different devices: /device:TPU:2 before, /device:TPU:0 now
where the time goes in v1:
time: 55.7 us; the launch traced here: 56.2 us
  waiting for transfers between devices  24.9 us (45%)
  Pallas kernels  23.7 us (43%)
  starting transfers between devices  7.31 us (13%)
    all_to_all x1, waiting for transfers between devices, per_device(): lax.all_to_all(sent.reshape(devices, local_rows * slots, channels), ('wav...  24.9 us
    pallas_call x1, Pallas kernels, fourier_stage(): pl.pallas_call(fourier_kernel, in_specs=[pl.BlockSpec(memory_space=pl.ANY...  9.46 us
    pallas_call x1, Pallas kernels, legendre_stage(): pl.pallas_call(lambda *refs: legendre_kernel(group, *refs), in_specs=[pl....  7.5 us
    all_to_all x1, starting transfers between devices, per_device(): lax.all_to_all(sent.reshape(devices, local_rows * slots, channels), ('wav...  7.31 us
    pallas_call x1, Pallas kernels, table_stage(): pl.pallas_call(table_kernel, grid=(local_rows,), in_specs=[pl.BlockSpec(m...  6.75 us
  transfers between devices with their start and end apart: 1, of which 1 were waited for; matrix products, arithmetic and copies ran while one was open for 0% of the time, Pallas kernels for 12%

profile of v1, /device:TPU:0, one launch (start us, length us, event | category | flops | bytes accessed | tf_op | source)
XLA Modules:
  0.0 56.2 jit_solution(3380920425429223810)
XLA Ops:
  0.0 0.0 copy-start.1
  0.0 0.0 copy-start
  0.0 7.5 %legendre.1 = f32[64,40,128]{2,1,0:T(8,128)} custom-call(s32[1280]{0:T(1024)} %refs_0_.1, bf16[40,64,1280]{2,1,0:T(8,128)(2,1)} %refs_1_.1, bf16[40,1280,128]{2,1,0:T(8,128)(2,1)} %refs_2_.1), custom_call_target="tpu_custom_call" | custom-call | tf_op jit(solution)/shard_map/legendre/pallas_call | solution.py:124
  7.5 7.3 %all-to-all-start = ((f32[32,80,128]{2,1,0:T(8,128)}), f32[32,80,128]{2,1,0:T(8,128)S(1)}, u32[]{:S(2)}, u32[]{:S(2)}) async-start(f32[32,80,128]{2,1,0:T(8,128)} %bitcast.3), calls=%async_computation | async-start | bytes 2621440 | tf_op jit(solution)/shard_map/all_to_all | solution.py:385
  14.8 0.0 copy-done.1
  14.9 0.0 copy-done
  14.9 0.2 broadcast_in_dim.5.row_waves_ref
  15.1 6.8 %trig_tables.1 = (bf16[2,2,2,1280,256]{4,3,2,1,0:T(8,128)(2,1)}, f32[2,2,16,1280]{3,2,1,0:T(8,128)}) custom-call(s32[2]{0:T(128)S(1)} %copy-done, f32[2]{0:T(128)S(1)} %convert_divide_fusion.inverse_ref, f32[8,1280]{1,0:T(8,128)S(1)} %broadcast_in_dim.4.lane_waves_ref, f32[1280,128]{1,0:T(8,128)S(1)} %broadcast_in_dim.5.row_waves_ref), custom_call_target="tpu_custom_call" | custom-call | flops 26214400 | bytes 5242880 | tf_op jit(solution)/shard_map/trig_tables/pallas_call | solution.py:184
  21.9 24.9 %all-to-all-done = f32[32,80,128]{2,1,0:T(8,128)S(1)} async-done(((f32[32,80,128]{2,1,0:T(8,128)}), f32[32,80,128]{2,1,0:T(8,128)S(1)}, u32[]{:S(2)}, u32[]{:S(2)}) %all-to-all-start) | async-done | bytes 1310752 | tf_op jit(solution)/shard_map/all_to_all | solution.py:385
  46.7 9.5 %fourier.1 = f32[2,64,5376]{2,1,0:T(8,128)} custom-call(s32[2]{0:T(128)S(1)} %copy-done, f32[32,2,40,128]{3,2,1,0:T(8,128)S(1)} %bitcast.2, bf16[2,2,2,1280,256]{4,3,2,1,0:T(8,128)(2,1)} %get-tuple-element.7.table_in_ref, f32[2,2,16,1280]{3,2,1,0:T(8,128)} %get-tuple-element.8.turn_in_ref), custom_call_target="tpu_custom_call" | custom-call | tf_op jit(solution)/shard_map/fourier/pallas_call | solution.py:344
  (3 shorter events, 0.0 us)
Async XLA Ops:
  0.0 14.8 %copy-start.1 = (s32[1280]{0:T(1024)S(1)}, s32[1280]{0:T(1024)}, u32[]{:S(2)}) copy-start(s32[1280]{0:T(1024)} %refs_0_.1) | copy-start | bytes 15364
  0.0 14.9 %copy-start = (s32[2]{0:T(128)S(1)}, s32[2]{0:T(128)}, u32[]{:S(2)}) copy-start(s32[2]{0:T(128)} %length_in_ref.1) | copy-start | bytes 28
  7.5 39.2 %all-to-all-start = ((f32[32,80,128]{2,1,0:T(8,128)}), f32[32,80,128]{2,1,0:T(8,128)S(1)}, u32[]{:S(2)}, u32[]{:S(2)}) async-start(f32[32,80,128]{2,1,0:T(8,128)} %bitcast.3), calls=%async_computation | async-start | bytes 2621440 | tf_op jit(solution)/shard_map/all_to_all | solution.py:385

commit v2 on v1

--- a/solution.py
+++ b/solution.py
@@ -14,7 +14,8 @@
 WHOLE = NLON // SPAN
 SKIP = 16
 PART = 8
-GROUP = 5
+LARGE = 10
+SMALL = 5
 TILE = 256
 MB = 1 << 20
 
@@ -213,21 +214,24 @@
     total_waves = senders * slots
     fields = channels // 2
     length_fetch = pltpu.make_async_copy(length_in_ref, length_ref, length_sem)
-    fetch_moved, fetch_turns, fetch_table = [], [], []
+    fetch_moved = []
     for row in range(local_rows):
         fetch_moved.append(pltpu.make_async_copy(moved_in_ref.at[:, row], moved_ref.at[:, row], in_sems.at[row, 0]))
-        fetch_turns.append(pltpu.make_async_copy(turn_in_ref.at[row], turn_ref.at[row], in_sems.at[row, 1]))
-        fetch_table.append(pltpu.make_async_copy(table_in_ref.at[row], table_ref.at[row], in_sems.at[row, 2]))
+
+    def fetch_turns(row):
+        return pltpu.make_async_copy(turn_in_ref.at[row], turn_ref.at[row], in_sems.at[row, 1])
+
+    def fetch_table(row):
+        return pltpu.make_async_copy(table_in_ref.at[row], table_ref.at[row], in_sems.at[row, 2])
+
+    def fetch_row(row):
+        fetch_turns(row).start()
+        fetch_table(row).start()
+
     length_fetch.start()
-
+    fetch_row(0)
     for row in range(local_rows):
         fetch_moved[row].start()
-
-    def fetch_row(row):
-        fetch_turns[row].start()
-        fetch_table[row].start()
-
-    fetch_row(0)
 
     def send(row, block):
         columns = pl.ds(pl.multiple_of(block * SPAN, SPAN), SPAN)
@@ -295,42 +299,47 @@
 
     length_fetch.wait()
     for row in range(local_rows):
+        fetch_moved[row].wait()
+        turn_row(row)
+
+    def one_row(row, carry):
         length = length_ref[row]
         block_count = (length + SPAN - 1) // SPAN
-        tail = lax.rem(block_count, GROUP) == 1
-        group_count = jnp.where(tail, block_count // GROUP, (block_count + GROUP - 1) // GROUP)
-        filled = jnp.minimum(group_count * GROUP + tail.astype(jnp.int32), WHOLE)
+        large = block_count // LARGE
+        rest = block_count - large * LARGE
+        large = jnp.where(rest > SMALL + 1, large + 1, large)
+        rest = jnp.where(rest > SMALL + 1, 0, rest)
+        small = jnp.where(rest > 1, 1, 0)
+        single = jnp.where((rest == 1) | (rest > SMALL), 1, 0)
+        filled = large * LARGE + small * SMALL + single
 
         def send_empty(block, carry):
             send(row, block).start()
             return carry
 
-        lax.fori_loop(filled, WHOLE, send_empty, 0)
-        if row == 0:
-            for each in range(local_rows):
-                fetch_moved[each].wait()
-                turn_row(each)
-        fetch_turns[row].wait()
-        fetch_table[row].wait()
-        if row + 1 < local_rows:
+        lax.fori_loop(jnp.minimum(filled, WHOLE), WHOLE, send_empty, 0)
+        fetch_turns(row).wait()
+        fetch_table(row).wait()
+
+        @pl.when(row + 1 < local_rows)
+        def _():
             fetch_row(row + 1)
 
-        def one_group(group, carry):
-            rotate(row, group * GROUP, GROUP)
-
-            transform(row, length, group * GROUP, GROUP)
-            return carry
-
-        lax.fori_loop(0, group_count, one_group, 0)
-
-        @pl.when(tail)
-        def _():
-            rotate(row, group_count * GROUP, 1)
-
-            transform(row, length, group_count * GROUP, 1)
-
+        def groups(first_block, count, size):
+            def one_group(group, carry):
+                rotate(row, first_block + group * size, size)
+                transform(row, length, first_block + group * size, size)
+                return carry
+
+            lax.fori_loop(0, count, one_group, 0)
+
+        groups(0, large, LARGE)
+        groups(large * LARGE, small, SMALL)
+        groups(large * LARGE + small * SMALL, single, 1)
         send_last(row).start()
-
+        return carry
+
+    lax.fori_loop(0, local_rows, one_row, 0)
     for row in range(local_rows):
         for block in range(WHOLE):
             send(row, block).wait()
@@ -359,8 +368,8 @@
             pltpu.VMEM((total_waves // 128, channels, 128), jnp.float32),
             pltpu.VMEM((local_rows, fields, total_waves), jnp.float32),
             pltpu.VMEM((local_rows, fields, total_waves), jnp.float32),
-            pltpu.VMEM((2, 2 * GROUP * fields, total_waves), jnp.bfloat16),
-            pltpu.VMEM((local_rows, fields, (BLOCKS + GROUP) * SPAN), jnp.float32),
+            pltpu.VMEM((2, 2 * LARGE * fields, total_waves), jnp.bfloat16),
+            pltpu.VMEM((local_rows, fields, (BLOCKS + LARGE) * SPAN), jnp.float32),
             pltpu.SemaphoreType.DMA,
             pltpu.SemaphoreType.DMA((local_rows, 3)),
             pltpu.SemaphoreType.DMA((local_rows, BLOCKS)),

time: 55.7 us -> 55.8 us (level); the launches traced: 56.2 us -> 54.9 us
  Pallas kernels: 23.7 us -> 21.8 us
  starting transfers between devices: 7.31 us -> 7.93 us
    pallas_call x1, Pallas kernels: 9.46 us -> 7.71 us  [fourier_stage(): pl.pallas_call(fourier_kernel, in_specs=[pl.BlockSpec(memory_space=pl.ANY...]
    all_to_all x1, starting transfers between devices: 7.31 us -> 7.93 us  [per_device(): lax.all_to_all(sent.reshape(devices, local_rows * slots, channels), ('wav...]
where the time goes in v2:
time: 55.8 us; the launch traced here: 54.9 us
  waiting for transfers between devices  24.9 us (45%)
  Pallas kernels  21.8 us (39%)
  starting transfers between devices  7.93 us (14%)
    all_to_all x1, waiting for transfers between devices, per_device(): lax.all_to_all(sent.reshape(devices, local_rows * slots, channels), ('wav...  24.9 us
    all_to_all x1, starting transfers between devices, per_device(): lax.all_to_all(sent.reshape(devices, local_rows * slots, channels), ('wav...  7.93 us
    pallas_call x1, Pallas kernels, fourier_stage(): pl.pallas_call(fourier_kernel, in_specs=[pl.BlockSpec(memory_space=pl.ANY...  7.71 us
    pallas_call x1, Pallas kernels, legendre_stage(): pl.pallas_call(lambda *refs: legendre_kernel(group, *refs), in_specs=[pl....  7.36 us
    pallas_call x1, Pallas kernels, table_stage(): pl.pallas_call(table_kernel, grid=(local_rows,), in_specs=[pl.BlockSpec(m...  6.75 us
  transfers between devices with their start and end apart: 1, of which 1 were waited for; matrix products, arithmetic and copies ran while one was open for 0% of the time, Pallas kernels for 12%

profile of v2, /device:TPU:0, one launch (start us, length us, event | category | flops | bytes accessed | tf_op | source)
XLA Modules:
  0.0 54.9 jit_solution(1466175882821059892)
XLA Ops:
  0.0 0.0 copy-start.1
  0.0 0.0 copy-start
  0.0 7.4 %legendre.1 = f32[64,40,128]{2,1,0:T(8,128)} custom-call(s32[1280]{0:T(1024)} %refs_0_.1, bf16[40,64,1280]{2,1,0:T(8,128)(2,1)} %refs_1_.1, bf16[40,1280,128]{2,1,0:T(8,128)(2,1)} %refs_2_.1), custom_call_target="tpu_custom_call" | custom-call | tf_op jit(solution)/shard_map/legendre/pallas_call | solution.py:125
  7.4 7.9 %all-to-all-start = ((f32[32,80,128]{2,1,0:T(8,128)}), f32[32,80,128]{2,1,0:T(8,128)S(1)}, u32[]{:S(2)}, u32[]{:S(2)}) async-start(f32[32,80,128]{2,1,0:T(8,128)} %bitcast.3), calls=%async_computation | async-start | bytes 2621440 | tf_op jit(solution)/shard_map/all_to_all | solution.py:394
  15.3 0.0 copy-done.1
  15.3 0.0 copy-done
  15.4 0.2 broadcast_in_dim.5.row_waves_ref
  15.6 6.8 %trig_tables.1 = (bf16[2,2,2,1280,256]{4,3,2,1,0:T(8,128)(2,1)}, f32[2,2,16,1280]{3,2,1,0:T(8,128)}) custom-call(s32[2]{0:T(128)S(1)} %copy-done, f32[2]{0:T(128)S(1)} %convert_divide_fusion.inverse_ref, f32[8,1280]{1,0:T(8,128)S(1)} %broadcast_in_dim.4.lane_waves_ref, f32[1280,128]{1,0:T(8,128)S(1)} %broadcast_in_dim.5.row_waves_ref), custom_call_target="tpu_custom_call" | custom-call | flops 26214400 | bytes 5242880 | tf_op jit(solution)/shard_map/trig_tables/pallas_call | solution.py:185
  22.4 24.9 %all-to-all-done = f32[32,80,128]{2,1,0:T(8,128)S(1)} async-done(((f32[32,80,128]{2,1,0:T(8,128)}), f32[32,80,128]{2,1,0:T(8,128)S(1)}, u32[]{:S(2)}, u32[]{:S(2)}) %all-to-all-start) | async-done | bytes 1310752 | tf_op jit(solution)/shard_map/all_to_all | solution.py:394
  47.2 7.7 %fourier.1 = f32[2,64,5376]{2,1,0:T(8,128)} custom-call(s32[2]{0:T(128)S(1)} %copy-done, f32[32,2,40,128]{3,2,1,0:T(8,128)S(1)} %bitcast.2, bf16[2,2,2,1280,256]{4,3,2,1,0:T(8,128)(2,1)} %get-tuple-element.7.table_in_ref, f32[2,2,16,1280]{3,2,1,0:T(8,128)} %get-tuple-element.8.turn_in_ref), custom_call_target="tpu_custom_call" | custom-call | tf_op jit(solution)/shard_map/fourier/pallas_call | solution.py:353
  (3 shorter events, 0.0 us)
Async XLA Ops:
  0.0 15.3 %copy-start.1 = (s32[1280]{0:T(1024)S(1)}, s32[1280]{0:T(1024)}, u32[]{:S(2)}) copy-start(s32[1280]{0:T(1024)} %refs_0_.1) | copy-start | bytes 15364
  0.0 15.3 %copy-start = (s32[2]{0:T(128)S(1)}, s32[2]{0:T(128)}, u32[]{:S(2)}) copy-start(s32[2]{0:T(128)} %length_in_ref.1) | copy-start | bytes 28
  7.4 39.8 %all-to-all-start = ((f32[32,80,128]{2,1,0:T(8,128)}), f32[32,80,128]{2,1,0:T(8,128)S(1)}, u32[]{:S(2)}, u32[]{:S(2)}) async-start(f32[32,80,128]{2,1,0:T(8,128)} %bitcast.3), calls=%async_computation | async-start | bytes 2621440 | tf_op jit(solution)/shard_map/all_to_all | solution.py:394
